TPU v7x, 512 devices: a whole 4x8x8 slice. The times are simulated.
512 devices in a mesh: leaf: 128 (over y, z, core), cols: 4 (over x).
Axes of the slice: x: 4, y: 8, z: 8, core: 2. Of those that a mesh axis runs over, the one named last changes fastest.
Arguments:
- samples: bfloat16 [262144, 256], P(('leaf', 'cols')), may hold values from -6 to 6
- near_tiles: bfloat16 [2048, 16, 128, 128], P('leaf', 'cols'), may hold values from -0.1875 to 0.1875
- columns: int32 [2048, 16], P('leaf', 'cols'), may hold values from 0 to 2047, as said below
- tile_count: int32 [2048], P('leaf'), may hold values from 4 to 16, as said below
- skeleton_one: int32 [16, 64, 128], P('cols'), may hold values from 0 to 255, as said below
- skeleton_two: int32 [16, 32, 128], P('cols'), may hold values from 0 to 255, as said below
- skeleton_three: int32 [16, 16, 128], P('cols'), may hold values from 0 to 255, as said below
Outputs:
- transfer_one: float32 [128, 8, 256, 128], P('leaf', 'cols')
- transfer_two: float32 [128, 4, 256, 128], P('leaf', 'cols')
- transfer_three: float32 [128, 4, 256, 128], P('leaf', 'cols')
- top_samples: float32 [128, 4, 128, 256], P('leaf', 'cols')
Inputs may be any that keep to these rules, and one draw needn't show every extreme that they name: `columns`: the column cluster of a slot of row cluster r, of any layer, lies in region r // 16 or a region beside it. `tile_count`: slots at or past a cluster's count are unused; some cluster uses all 16. `skeleton_one`: each row holds 128 distinct indices. `skeleton_two`: each row holds 128 distinct indices. `skeleton_three`: each row holds 128 distinct indices.
All inputs are finite; a program needn't handle non-finite values.
Results may differ from a plain program's by a relative error of at most 0.0003.
Values may be sent and summed in bfloat16 or wider, within the bound.
No kernel may reach another device: no remote copies, remote signals or barrier semaphores. Data moves between devices by JAX's collectives and lax.ppermute only.
A program may use at most 64 MiB of HBM per device.

v0:
```python
import jax
import jax.numpy as jnp
from jax import lax
from jax.sharding import PartitionSpec as P

HIGHEST = lax.Precision.HIGHEST
RIDGE = 0.25


def padded(value, sides, width):
    for axis, dim in sides:
        count, length = (lax.axis_size(axis), value.shape[dim])
        up = [(i, (i + 1) % count) for i in range(count - 1)]
        down = [(j, i) for i, j in up]
        last = lax.slice_in_dim(value, length - width, length, axis=dim)
        initial = lax.slice_in_dim(value, 0, width, axis=dim)
        before = lax.ppermute(last, axis, up)
        after = lax.ppermute(initial, axis, down)
        value = jnp.concatenate([before, value, after], axis=dim)
    return value


def swapped(block, axis, apart):
    count = lax.axis_size(axis)
    route = []
    for low in range(count):
        high = low | 1 << apart
        if high != low and high < count:
            route += [(low, high), (high, low)]
    return lax.ppermute(block, axis, route)


def merge_pair(first, second, chosen):
    stacked = jnp.concatenate([first, second], axis=1)
    picked = jax.vmap(lambda block, index: block[index])(stacked, chosen)
    count = stacked.shape[2]
    rank = picked.shape[1]
    gram = jnp.einsum("mis,mjs->mij", picked, picked, precision=HIGHEST) / count
    gram = gram + RIDGE * jnp.eye(rank, dtype=jnp.float32)
    lower = jnp.linalg.cholesky(gram)
    basis = jax.vmap(
        lambda factor, rhs: jax.scipy.linalg.solve_triangular(factor, rhs, lower=True)
    )(lower, picked)
    transfer = jnp.einsum("mis,mjs->mij", stacked, basis, precision=HIGHEST) / count
    return (basis, transfer)


def local(samples, near_tiles, columns, tile_count, skeleton_one, skeleton_two, skeleton_three):
    leaf_index = lax.axis_index("leaf")
    cols_index = lax.axis_index("cols")
    clusters, slots, panels, _ = near_tiles.shape
    width = samples.shape[1]
    own_rows = lax.all_gather(samples, "cols", axis=0, tiled=True)
    near_rows = padded(own_rows, (("leaf", 0),), own_rows.shape[0])
    window = near_rows.reshape(3 * clusters, panels, width)
    local_cols = columns - (leaf_index - 1) * clusters
    picked = jnp.take(window, local_cols, axis=0)
    slot_ids = cols_index * slots + lax.iota(jnp.int32, slots)
    active = (slot_ids[None, :] < tile_count[:, None]).astype(picked.dtype)
    picked = picked * active[:, :, None, None]
    partial_value = jnp.einsum(
        "ksij,ksjn->kin", near_tiles, picked, preferred_element_type=jnp.float32
    )
    nodes = lax.psum_scatter(partial_value, "cols", scatter_dimension=0, tiled=True)
    subtrees = nodes.shape[0]
    outputs = []
    level = 0
    spread = 1
    for skeleton in (skeleton_one, skeleton_two, skeleton_three):
        level = level + 1
        side = leaf_index >> level - 1 & 1
        group = leaf_index >> level
        spread = min(2**level, subtrees)
        offset = leaf_index % spread
        chosen_all = lax.dynamic_index_in_dim(skeleton, group, axis=1, keepdims=False)
        other = swapped(nodes, "leaf", level - 1)
        first = jnp.where(side == 0, nodes, other)
        second = jnp.where(side == 0, other, nodes)
        basis, transfer = merge_pair(first, second, chosen_all)
        kept = lax.dynamic_index_in_dim(
            transfer.reshape(subtrees // spread, spread, 2 * panels, panels),
            offset,
            axis=1,
            keepdims=False,
        )
        outputs.append(kept[None])
        nodes = basis
    offset = leaf_index % spread
    top = lax.dynamic_index_in_dim(
        nodes.reshape(subtrees // spread, spread, panels, width), offset, axis=1, keepdims=False
    )
    return (outputs[0], outputs[1], outputs[2], top[None])


def solution(mesh):
    placed = (
        P(("leaf", "cols"), None),
        P("leaf", "cols", None, None),
        P("leaf", "cols"),
        P("leaf"),
        P("cols", None, None),
        P("cols", None, None),
        P("cols", None, None),
    )
    return jax.shard_map(
        local,
        mesh=mesh,
        in_specs=placed,
        out_specs=(
            P("leaf", "cols", None, None),
            P("leaf", "cols", None, None),
            P("leaf", "cols", None, None),
            P("leaf", "cols", None, None),
        ),
        check_vma=False,
    )
```

profile of v0, /device:TPU:8, one launch (start us, length us, event | category | flops | bytes accessed | tf_op | source)
XLA Modules:
  0.0 481.1 jit_solution(7024307054163040325)
XLA Ops:
  8.0 36.0 %all-gather.2.cloned.1.call-done = bf16[2048,256]{1,0:T(8,128)(2,1)} async-done(((bf16[512,256]{1,0:T(8,128)(2,1)}), bf16[2048,256]{1,0:T(8,128)(2,1)}) %all-gather.2.cloned.1.call-update) | async-done | bytes 1048592 | tf_op jit(solution)/shard_map/all_gather | solution.py:53
  45.9 5.8 %collective-permute-start.1 = (bf16[2048,256]{1,0:T(8,128)(2,1)}, bf16[2048,256]{1,0:T(8,128)(2,1)}, u32[]{:S(2)}, u32[]{:S(2)}) collective-permute-start(bf16[2048,256]{1,0:T(8,128)(2,1)} %all-gather.2.cloned.1.call-done), channel_id=1, source_target_pairs={{4,0},{8,4},{12,8},{16,12},{20,16},{24,20},{28,24},{32,28},{36,32}... | collective-permute-start | bytes 3145736 | tf_op jit(solution)/shard_map/ppermute | solution.py:18
  53.4 9.0 %collective-permute-done = bf16[2048,256]{1,0:T(8,128)(2,1)S(1)} collective-permute-done((bf16[2048,256]{1,0:T(8,128)(2,1)}, bf16[2048,256]{1,0:T(8,128)(2,1)S(1)}, u32[]{:S(2)}, u32[]{:S(2)}) %collective-permute-start) | collective-permute-done | bytes 1048608 | tf_op jit(solution)/shard_map/ppermute | solution.py:17
  64.3 3.0 pad_maximum_fusion
  67.3 4.6 gather_fusion
  71.9 6.4 %copy.41 = bf16[64,128,256]{1,2,0:T(8,128)(2,1)} copy(bf16[64,128,256]{2,1,0:T(8,128)(2,1)} %gather_fusion) | data formatting | bytes 8388608 | tf_op jit(solution)/shard_map/jit(_take)/gather | solution.py:57
  78.3 4.8 %fusion.6 = f32[16,128,256]{1,2,0:T(8,128)} fusion(bf16[16,4,128,128]{3,2,1,0:T(8,128)(2,1)S(1)} %copy-done, bf16[16,4,128,256]{2,3,1,0:T(8,128)(2,1)} %bitcast.75, pred[16,4]{1,0:T(8,128)(4,1)S(1)} %copy.39, bf16[16,4]{1,0:T(8,128)(2,1)S(1)} %compare_convert_fusion), kind=kOutput, calls=%fused_computation.11 | convolution fusion | flops 541065216 | bytes 8388800 | tf_op jit(solution)/shard_map/ksij,ksjn->kin/dot_general | solution.py:61
  84.0 34.4 %reduce-scatter.2.cloned.1.call-done = f32[4,128,256]{1,2,0:T(8,128)} async-done(((f32[16,128,256]{1,2,0:T(8,128)}), f32[4,128,256]{1,2,0:T(8,128)}) %reduce-scatter.2.cloned.1.call-update) | async-done | bytes 524304 | tf_op jit(solution)/shard_map/reduce_scatter | solution.py:64
  127.0 6.3 %gather_fusion.1 = f32[512,256]{1,0:T(8,128)} fusion(f32[4,256,256]{2,1,0:T(8,128)S(1)} %copy.42, s32[512]{0:T(512)S(1)} %get-tuple-element.14), kind=kCustom, calls=%fused_computation.1 | custom fusion | bytes 1052672 | tf_op jit(solution)/shard_map/vmap()/gather | solution.py:35
  135.4 46.9 %custom-call.16 = f32[4,128,128]{2,1,0:T(8,128)S(1)} custom-call(f32[4,128,128]{2,1,0:T(8,128)S(1)} %fusion.20), custom_call_target="Cholesky" | custom-call | tf_op jit(solution)/shard_map/jit(cholesky)/cholesky | solution.py:40
  182.6 39.3 %custom-call.17 = f32[4,1,128,128]{2,3,1,0:T(8,128)S(1)} custom-call(f32[4,1,128,128]{3,2,1,0:T(8,128)S(1)} %select_bitcast_fusion.2), custom_call_target="InvertDiagBlocksLowerTriangular" | custom-call | tf_op jit(solution)/shard_map/vmap(jit(_solve_triangular))/triangular_solve | solution.py:42
  223.6 3.8 collective-permute-start.3
  228.1 11.3 %collective-permute-done.3 = f32[4,128,256]{2,1,0:T(8,128)S(1)} collective-permute-done((f32[4,128,256]{2,1,0:T(8,128)S(1)}, f32[4,128,256]{2,1,0:T(8,128)S(1)}, u32[]{:S(2)}, u32[]{:S(2)}) %collective-permute-start.3) | collective-permute-done | bytes 524320 | tf_op jit(solution)/shard_map/ppermute | solution.py:30
  240.5 6.4 %gather_fusion.2 = f32[512,256]{1,0:T(8,128)} fusion(f32[4,256,256]{2,1,0:T(8,128)S(1)} %pad_maximum_fusion.2, s32[512]{0:T(512)S(1)} %get-tuple-element.15), kind=kCustom, calls=%fused_computation.2 | custom fusion | bytes 1052672 | tf_op jit(solution)/shard_map/vmap()/gather | solution.py:35
  246.9 1.9 fusion.10
  251.3 47.7 %custom-call.18 = f32[4,128,128]{2,1,0:T(8,128)S(1)} custom-call(f32[4,128,128]{2,1,0:T(8,128)} %fusion.17), custom_call_target="Cholesky" | custom-call | tf_op jit(solution)/shard_map/jit(cholesky)/cholesky | solution.py:40
  300.0 40.1 %custom-call.19 = f32[4,1,128,128]{2,3,1,0:T(8,128)S(1)} custom-call(f32[4,1,128,128]{3,2,1,0:T(8,128)} %select_bitcast_fusion.1), custom_call_target="InvertDiagBlocksLowerTriangular" | custom-call | tf_op jit(solution)/shard_map/vmap(jit(_solve_triangular))/triangular_solve | solution.py:42
  341.9 4.7 collective-permute-start.4
  346.6 2.9 convolution_multiply_fusion
  352.0 17.2 %collective-permute-done.4 = f32[4,128,256]{2,1,0:T(8,128)S(1)} collective-permute-done((f32[4,128,256]{2,1,0:T(8,128)S(1)}, f32[4,128,256]{2,1,0:T(8,128)S(1)}, u32[]{:S(2)}, u32[]{:S(2)}) %collective-permute-start.4) | collective-permute-done | bytes 524320 | tf_op jit(solution)/shard_map/ppermute | solution.py:30
  370.4 6.6 %gather_fusion.3 = f32[512,256]{1,0:T(8,128)} fusion(f32[4,256,256]{2,1,0:T(8,128)S(1)} %pad_maximum_fusion.3, s32[512]{0:T(512)S(1)} %fusion.35), kind=kCustom, calls=%fused_computation.3 | custom fusion | bytes 1052672 | tf_op jit(solution)/shard_map/vmap()/gather | solution.py:35
  377.0 1.9 fusion.11
  381.4 47.7 %custom-call.20 = f32[4,128,128]{2,1,0:T(8,128)S(1)} custom-call(f32[4,128,128]{2,1,0:T(8,128)} %fusion.14), custom_call_target="Cholesky" | custom-call | tf_op jit(solution)/shard_map/jit(cholesky)/cholesky | solution.py:40
  430.0 40.1 %custom-call.21 = f32[4,1,128,128]{2,3,1,0:T(8,128)S(1)} custom-call(f32[4,1,128,128]{3,2,1,0:T(8,128)} %select_bitcast_fusion), custom_call_target="InvertDiagBlocksLowerTriangular" | custom-call | tf_op jit(solution)/shard_map/vmap(jit(_solve_triangular))/triangular_solve | solution.py:42
  (83 shorter events, 37.8 us)
Async XLA Ops:
  7.2 71.2 %copy-start = (bf16[16,4,128,128]{3,2,1,0:T(8,128)(2,1)S(1)}, bf16[16,4,128,128]{3,2,1,0:T(8,128)(2,1)}, u32[]{:S(2)}) copy-start(bf16[16,4,128,128]{3,2,1,0:T(8,128)(2,1)} %param.11) | copy-start | bytes 6291460
  7.2 36.8 %all-gather.2.cloned.1.call-start = ((), (), s32[]{:S(2)}) async-start(), calls=%async_computation.1 | async-start | bytes 1310720 | tf_op jit(solution)/shard_map/all_gather | solution.py:53
  7.9 110.4 %reduce-scatter.2.cloned.1.call-start = ((), (), s32[]{:S(2)}) async-start(), calls=%async_computation.2 | async-start | bytes 2621440 | tf_op jit(solution)/shard_map/reduce_scatter | solution.py:64
  44.0 18.4 %collective-permute-start = (bf16[2048,256]{1,0:T(8,128)(2,1)}, bf16[2048,256]{1,0:T(8,128)(2,1)S(1)}, u32[]{:S(2)}, u32[]{:S(2)}) collective-permute-start(bf16[2048,256]{1,0:T(8,128)(2,1)} %all-gather.2.cloned.1.call-done), channel_id=1, source_target_pairs={{0,4},{4,8},{8,12},{12,16},{16,20},{20,24},{24,28},{28,32},{32,36}... | collective-permute-start | bytes 3145736 | tf_op jit(solution)/shard_map/ppermute | solution.py:17
  45.9 18.4 %collective-permute-start.1 = (bf16[2048,256]{1,0:T(8,128)(2,1)}, bf16[2048,256]{1,0:T(8,128)(2,1)}, u32[]{:S(2)}, u32[]{:S(2)}) collective-permute-start(bf16[2048,256]{1,0:T(8,128)(2,1)} %all-gather.2.cloned.1.call-done), channel_id=1, source_target_pairs={{4,0},{8,4},{12,8},{16,12},{20,16},{24,20},{28,24},{32,28},{36,32}... | collective-permute-start | bytes 3145736 | tf_op jit(solution)/shard_map/ppermute | solution.py:18
  118.3 4.0 collective-permute-start.2
  123.4 0.8 copy-start.3
  123.4 1.0 copy-start.5
  223.6 16.0 %copy-start.1 = (f32[4,128,256]{2,1,0:T(8,128)}, f32[4,128,256]{2,1,0:T(8,128)S(1)}, u32[]{:S(2)}) copy-start(f32[4,128,256]{2,1,0:T(8,128)S(1)} %fusion.18) | copy-start | bytes 1572868
  223.6 15.9 %collective-permute-start.3 = (f32[4,128,256]{2,1,0:T(8,128)S(1)}, f32[4,128,256]{2,1,0:T(8,128)S(1)}, u32[]{:S(2)}, u32[]{:S(2)}) collective-permute-start(f32[4,128,256]{2,1,0:T(8,128)S(1)} %fusion.18), channel_id=1, source_target_pairs={{0,8},{8,0},{4,12},{12,4},{16,24},{24,16},{20,28},{28,20},{32,40},... | collective-permute-start | bytes 1572872 | tf_op jit(solution)/shard_map/ppermute | solution.py:30
  239.6 0.8 copy-start.6
  239.6 1.0 copy-start.8
  246.9 99.7 %copy-start.2 = (f32[4,128,256]{2,1,0:T(8,128)S(1)}, f32[4,128,256]{2,1,0:T(8,128)}, u32[]{:S(2)}) copy-start(f32[4,128,256]{2,1,0:T(8,128)} %copy-done.1) | copy-start | bytes 1572868
  246.9 99.7 %copy-start.4 = (f32[4,128,256]{1,2,0:T(8,128)S(1)}, f32[4,128,256]{1,2,0:T(8,128)}, u32[]{:S(2)}) copy-start(f32[4,128,256]{1,2,0:T(8,128)} %copy-done.3) | copy-start | bytes 1572868
  340.1 10.1 %copy-start.7 = (f32[4,128,256]{2,1,0:T(8,128)S(1)}, f32[4,128,256]{2,1,0:T(8,128)}, u32[]{:S(2)}) copy-start(f32[4,128,256]{2,1,0:T(8,128)} %copy-done.6) | copy-start | bytes 1572868
  340.1 10.1 %copy-start.9 = (f32[4,128,256]{2,1,0:T(8,128)S(1)}, f32[4,128,256]{2,1,0:T(8,128)}, u32[]{:S(2)}) copy-start(f32[4,128,256]{2,1,0:T(8,128)} %copy-done.8) | copy-start | bytes 1572868
  341.9 27.3 %collective-permute-start.4 = (f32[4,128,256]{2,1,0:T(8,128)S(1)}, f32[4,128,256]{2,1,0:T(8,128)S(1)}, u32[]{:S(2)}, u32[]{:S(2)}) collective-permute-start(f32[4,128,256]{2,1,0:T(8,128)S(1)} %fusion.15), channel_id=1, source_target_pairs={{0,16},{16,0},{4,20},{20,4},{8,24},{24,8},{12,28},{28,12},{32,48},... | collective-permute-start | bytes 1572872 | tf_op jit(solution)/shard_map/ppermute | solution.py:30
  369.3 0.8 copy-start.10
  369.3 1.0 copy-start.12
  376.9 94.9 %copy-start.11 = (f32[4,128,256]{2,1,0:T(8,128)S(1)}, f32[4,128,256]{2,1,0:T(8,128)}, u32[]{:S(2)}) copy-start(f32[4,128,256]{2,1,0:T(8,128)} %copy-done.10) | copy-start | bytes 1572868
  376.9 94.9 %copy-start.13 = (f32[4,128,256]{2,1,0:T(8,128)S(1)}, f32[4,128,256]{2,1,0:T(8,128)}, u32[]{:S(2)}) copy-start(f32[4,128,256]{2,1,0:T(8,128)} %copy-done.12) | copy-start | bytes 1572868
Sparse Core Ops, SparseCore 0:
  10.1 33.8 all-gather.1
  83.3 34.9 reduce-scatter.1
where the time goes:
time: 482 us; the launch traced here: 481 us
  other arithmetic  276 us (57%)
  waiting for transfers between devices  112 us (23%)
  local copies, waits for them, and re-layouts  40.4 us (8%)
  matrix products  20.6 us (4%)
  starting transfers between devices  18.1 us (4%)
  between operations  14.5 us (3%)
    another operation x10, other arithmetic, merge_pair(): lower = jnp.linalg.cholesky(gram)  143 us
    another operation x7, other arithmetic, merge_pair(): jax.scipy.linalg.solve_triangular(factor, rhs, lower=True)  121 us
    all_gather x1, waiting for transfers between devices, local(): own_rows = lax.all_gather(samples, 'cols', axis=0, tiled=True)  36 us
    reduce_scatter x1, waiting for transfers between devices, local(): lax.psum_scatter(partial_value, 'cols', scatter_dimension=0, tiled=True)  34.4 us
    ppermute x3, waiting for transfers between devices, swapped(): return lax.ppermute(block, axis, route)  29.8 us
    gather x3, local copies, waits for them, and re-layouts, merge_pair(): picked = jax.vmap(lambda block, index: block[index])(stacked, chosen)  19.3 us
    gather x2, local copies, waits for them, and re-layouts, local(): picked = jnp.take(window, local_cols, axis=0)  11.1 us
    ppermute x3, starting transfers between devices, swapped(): return lax.ppermute(block, axis, route)  10.3 us
  transfers between devices with their start and end apart: 7, of which 7 were waited for; matrix products, arithmetic and copies ran while one was open for 2% of the time, Pallas kernels for 0%

commit v1 on v0

--- a/solution.py
+++ b/solution.py
@@ -50,7 +50,12 @@
     cols_index = lax.axis_index("cols")
     clusters, slots, panels, _ = near_tiles.shape
     width = samples.shape[1]
-    own_rows = lax.all_gather(samples, "cols", axis=0, tiled=True)
+    gallery = []
+    chips = lax.axis_size("cols")
+    for dev_j in tuple(range(samples.ndim)):
+        gallery.append(chips if dev_j == 0 else 1)
+    y2 = jnp.tile(samples, gallery)
+    own_rows = lax.all_to_all(y2, axis_name="cols", tiled=True, split_axis=0, concat_axis=0)
     near_rows = padded(own_rows, (("leaf", 0),), own_rows.shape[0])
     window = near_rows.reshape(3 * clusters, panels, width)
     local_cols = columns - (leaf_index - 1) * clusters

time: 482 us -> 468 us (0.971)
  waiting for transfers between devices: 112 us -> 73.8 us
  blocking collectives: 0 us -> 19.2 us
    all_gather x1 -> x0, waiting for transfers between devices: 36 us -> none  [local(): own_rows = lax.all_gather(samples, 'cols', axis=0, tiled=True)]
    all_to_all x0 -> x1, blocking collectives: none -> 19.2 us  [local(): lax.all_to_all(y2, axis_name='cols', tiled=True, split_axis=0, concat_axi...]
  transfers between devices with their start and end apart: 7 -> 6, of which waited for: 7 -> 6; matrix products, arithmetic and copies ran while one was open for 2% -> 2% of each run, Pallas kernels for 0% -> 0%
where the time goes in v1:
time: 468 us; the launch traced here: 467 us
  other arithmetic  276 us (59%)
  waiting for transfers between devices  73.8 us (16%)
  local copies, waits for them, and re-layouts  41.7 us (9%)
  starting transfers between devices  21.3 us (5%)
  matrix products  20.6 us (4%)
  blocking collectives  19.2 us (4%)
  between operations  14.5 us (3%)
    another operation x10, other arithmetic, merge_pair(): lower = jnp.linalg.cholesky(gram)  143 us
    another operation x7, other arithmetic, merge_pair(): jax.scipy.linalg.solve_triangular(factor, rhs, lower=True)  121 us
    reduce_scatter x1, waiting for transfers between devices, local(): lax.psum_scatter(partial_value, 'cols', scatter_dimension=0, tiled=True)  33.4 us
    ppermute x3, waiting for transfers between devices, swapped(): return lax.ppermute(block, axis, route)  29.8 us
    gather x3, local copies, waits for them, and re-layouts, merge_pair(): picked = jax.vmap(lambda block, index: block[index])(stacked, chosen)  19.3 us
    all_to_all x1, blocking collectives, local(): lax.all_to_all(y2, axis_name='cols', tiled=True, split_axis=0, concat_axi...  19.2 us
    gather x2, local copies, waits for them, and re-layouts, local(): picked = jnp.take(window, local_cols, axis=0)  11.1 us
    ppermute x3, starting transfers between devices, swapped(): return lax.ppermute(block, axis, route)  10.3 us
  transfers between devices with their start and end apart: 6, of which 6 were waited for; matrix products, arithmetic and copies ran while one was open for 2% of the time, Pallas kernels for 0%

profile of v1, /device:TPU:8, one launch (start us, length us, event | category | flops | bytes accessed | tf_op | source)
XLA Modules:
  0.0 466.9 jit_solution(1200284552215082906)
XLA Ops:
  8.4 19.2 %all_to_all.9 = bf16[4,512,256]{2,1,0:T(8,128)(2,1)S(1)} all-to-all(bf16[4,512,256]{2,1,0:T(8,128)(2,1)S(1)} %tile.2), channel_id=1, replica_groups=mesh['leaf'=128,'cols'=4] {'cols'}, dimensions={0} | all-to-all | bytes 2097152 | tf_op jit(solution)/shard_map/all_to_all | solution.py:58
  29.5 9.1 %collective-permute-start.1 = (bf16[2048,256]{1,0:T(8,128)(2,1)S(1)}, bf16[2048,256]{1,0:T(8,128)(2,1)}, u32[]{:S(2)}, u32[]{:S(2)}) collective-permute-start(bf16[2048,256]{1,0:T(8,128)(2,1)S(1)} %bitcast.78), channel_id=1, source_target_pairs={{4,0},{8,4},{12,8},{16,12},{20,16},{24,20},{28,24},{32,28},{36,32}... | collective-permute-start | bytes 3145736 | tf_op jit(solution)/shard_map/ppermute | solution.py:18
  40.3 8.9 %collective-permute-done = bf16[2048,256]{1,0:T(8,128)(2,1)} collective-permute-done((bf16[2048,256]{1,0:T(8,128)(2,1)S(1)}, bf16[2048,256]{1,0:T(8,128)(2,1)}, u32[]{:S(2)}, u32[]{:S(2)}) %collective-permute-start) | collective-permute-done | bytes 1048608 | tf_op jit(solution)/shard_map/ppermute | solution.py:17
  50.9 3.0 pad_maximum_fusion
  53.9 4.6 gather_fusion
  58.5 6.4 %copy.40 = bf16[16,4,128,256]{2,3,1,0:T(8,128)(2,1)} copy(bf16[16,4,128,256]{3,2,1,0:T(8,128)(2,1)} %bitcast.70) | data formatting | bytes 8388608 | tf_op jit(solution)/shard_map/jit(_take)/gather | solution.py:62
  64.9 4.8 %fusion.6 = f32[16,128,256]{1,2,0:T(8,128)} fusion(bf16[16,4,128,128]{3,2,1,0:T(8,128)(2,1)S(1)} %copy-done, bf16[16,4,128,256]{2,3,1,0:T(8,128)(2,1)} %copy.40, pred[16,4]{1,0:T(8,128)(4,1)S(1)} %copy.38, bf16[16,4]{1,0:T(8,128)(2,1)S(1)} %compare_convert_fusion), kind=kOutput, calls=%fused_computation.11 | convolution fusion | flops 541065216 | bytes 8388800 | tf_op jit(solution)/shard_map/ksij,ksjn->kin/dot_general | solution.py:66
  70.6 33.4 %reduce-scatter.2.cloned.1.call-done = f32[4,128,256]{1,2,0:T(8,128)} async-done(((f32[16,128,256]{1,2,0:T(8,128)}), f32[4,128,256]{1,2,0:T(8,128)}) %reduce-scatter.2.cloned.1.call-update) | async-done | bytes 524304 | tf_op jit(solution)/shard_map/reduce_scatter | solution.py:69
  112.8 6.4 %gather_fusion.1 = f32[512,256]{1,0:T(8,128)} fusion(f32[4,256,256]{2,1,0:T(8,128)S(1)} %copy.41, s32[512]{0:T(512)S(1)} %get-tuple-element.14), kind=kCustom, calls=%fused_computation.1 | custom fusion | bytes 1052672 | tf_op jit(solution)/shard_map/vmap()/gather | solution.py:35
  121.1 46.9 %custom-call.16 = f32[4,128,128]{2,1,0:T(8,128)S(1)} custom-call(f32[4,128,128]{2,1,0:T(8,128)S(1)} %fusion.20), custom_call_target="Cholesky" | custom-call | tf_op jit(solution)/shard_map/jit(cholesky)/cholesky | solution.py:40
  168.3 39.3 %custom-call.17 = f32[4,1,128,128]{2,3,1,0:T(8,128)S(1)} custom-call(f32[4,1,128,128]{3,2,1,0:T(8,128)S(1)} %select_bitcast_fusion.2), custom_call_target="InvertDiagBlocksLowerTriangular" | custom-call | tf_op jit(solution)/shard_map/vmap(jit(_solve_triangular))/triangular_solve | solution.py:42
  209.3 3.8 collective-permute-start.3
  213.9 11.3 %collective-permute-done.3 = f32[4,128,256]{2,1,0:T(8,128)S(1)} collective-permute-done((f32[4,128,256]{2,1,0:T(8,128)S(1)}, f32[4,128,256]{2,1,0:T(8,128)S(1)}, u32[]{:S(2)}, u32[]{:S(2)}) %collective-permute-start.3) | collective-permute-done | bytes 524320 | tf_op jit(solution)/shard_map/ppermute | solution.py:30
  226.3 6.4 %gather_fusion.2 = f32[512,256]{1,0:T(8,128)} fusion(f32[4,256,256]{2,1,0:T(8,128)S(1)} %pad_maximum_fusion.2, s32[512]{0:T(512)S(1)} %get-tuple-element.15), kind=kCustom, calls=%fused_computation.2 | custom fusion | bytes 1052672 | tf_op jit(solution)/shard_map/vmap()/gather | solution.py:35
  232.6 1.9 fusion.10
  237.1 47.7 %custom-call.18 = f32[4,128,128]{2,1,0:T(8,128)S(1)} custom-call(f32[4,128,128]{2,1,0:T(8,128)} %fusion.17), custom_call_target="Cholesky" | custom-call | tf_op jit(solution)/shard_map/jit(cholesky)/cholesky | solution.py:40
  285.8 40.1 %custom-call.19 = f32[4,1,128,128]{2,3,1,0:T(8,128)S(1)} custom-call(f32[4,1,128,128]{3,2,1,0:T(8,128)} %select_bitcast_fusion.1), custom_call_target="InvertDiagBlocksLowerTriangular" | custom-call | tf_op jit(solution)/shard_map/vmap(jit(_solve_triangular))/triangular_solve | solution.py:42
  327.7 4.6 collective-permute-start.4
  332.4 2.9 convolution_multiply_fusion
  337.8 17.2 %collective-permute-done.4 = f32[4,128,256]{2,1,0:T(8,128)S(1)} collective-permute-done((f32[4,128,256]{2,1,0:T(8,128)S(1)}, f32[4,128,256]{2,1,0:T(8,128)S(1)}, u32[]{:S(2)}, u32[]{:S(2)}) %collective-permute-start.4) | collective-permute-done | bytes 524320 | tf_op jit(solution)/shard_map/ppermute | solution.py:30
  356.1 6.6 %gather_fusion.3 = f32[512,256]{1,0:T(8,128)} fusion(f32[4,256,256]{2,1,0:T(8,128)S(1)} %pad_maximum_fusion.3, s32[512]{0:T(512)S(1)} %fusion.35), kind=kCustom, calls=%fused_computation.3 | custom fusion | bytes 1052672 | tf_op jit(solution)/shard_map/vmap()/gather | solution.py:35
  362.7 1.9 fusion.11
  367.1 47.7 %custom-call.20 = f32[4,128,128]{2,1,0:T(8,128)S(1)} custom-call(f32[4,128,128]{2,1,0:T(8,128)} %fusion.14), custom_call_target="Cholesky" | custom-call | tf_op jit(solution)/shard_map/jit(cholesky)/cholesky | solution.py:40
  415.8 40.1 %custom-call.21 = f32[4,1,128,128]{2,3,1,0:T(8,128)S(1)} custom-call(f32[4,1,128,128]{3,2,1,0:T(8,128)} %select_bitcast_fusion), custom_call_target="InvertDiagBlocksLowerTriangular" | custom-call | tf_op jit(solution)/shard_map/vmap(jit(_solve_triangular))/triangular_solve | solution.py:42
  (82 shorter events, 38.0 us)
Async XLA Ops:
  7.2 57.8 %copy-start = (bf16[16,4,128,128]{3,2,1,0:T(8,128)(2,1)S(1)}, bf16[16,4,128,128]{3,2,1,0:T(8,128)(2,1)}, u32[]{:S(2)}) copy-start(bf16[16,4,128,128]{3,2,1,0:T(8,128)(2,1)} %param.11) | copy-start | bytes 6291460
  7.2 96.8 %reduce-scatter.2.cloned.1.call-start = ((), (), s32[]{:S(2)}) async-start(), calls=%async_computation.2 | async-start | bytes 2621440 | tf_op jit(solution)/shard_map/reduce_scatter | solution.py:69
  27.6 21.7 %collective-permute-start = (bf16[2048,256]{1,0:T(8,128)(2,1)S(1)}, bf16[2048,256]{1,0:T(8,128)(2,1)}, u32[]{:S(2)}, u32[]{:S(2)}) collective-permute-start(bf16[2048,256]{1,0:T(8,128)(2,1)S(1)} %bitcast.77), channel_id=1, source_target_pairs={{0,4},{4,8},{8,12},{12,16},{16,20},{20,24},{24,28},{28,32},{32,36}... | collective-permute-start | bytes 3145736 | tf_op jit(solution)/shard_map/ppermute | solution.py:17
  29.5 21.4 %collective-permute-start.1 = (bf16[2048,256]{1,0:T(8,128)(2,1)S(1)}, bf16[2048,256]{1,0:T(8,128)(2,1)}, u32[]{:S(2)}, u32[]{:S(2)}) collective-permute-start(bf16[2048,256]{1,0:T(8,128)(2,1)S(1)} %bitcast.78), channel_id=1, source_target_pairs={{4,0},{8,4},{12,8},{16,12},{20,16},{24,20},{28,24},{32,28},{36,32}... | collective-permute-start | bytes 3145736 | tf_op jit(solution)/shard_map/ppermute | solution.py:18
  104.0 4.0 collective-permute-start.2
  109.1 0.8 copy-start.3
  109.1 1.0 copy-start.5
  209.3 16.0 %copy-start.1 = (f32[4,128,256]{2,1,0:T(8,128)}, f32[4,128,256]{2,1,0:T(8,128)S(1)}, u32[]{:S(2)}) copy-start(f32[4,128,256]{2,1,0:T(8,128)S(1)} %fusion.18) | copy-start | bytes 1572868
  209.3 15.9 %collective-permute-start.3 = (f32[4,128,256]{2,1,0:T(8,128)S(1)}, f32[4,128,256]{2,1,0:T(8,128)S(1)}, u32[]{:S(2)}, u32[]{:S(2)}) collective-permute-start(f32[4,128,256]{2,1,0:T(8,128)S(1)} %fusion.18), channel_id=1, source_target_pairs={{0,8},{8,0},{4,12},{12,4},{16,24},{24,16},{20,28},{28,20},{32,40},... | collective-permute-start | bytes 1572872 | tf_op jit(solution)/shard_map/ppermute | solution.py:30
  225.3 0.8 copy-start.6
  225.3 1.0 copy-start.8
  232.6 99.7 %copy-start.2 = (f32[4,128,256]{2,1,0:T(8,128)S(1)}, f32[4,128,256]{2,1,0:T(8,128)}, u32[]{:S(2)}) copy-start(f32[4,128,256]{2,1,0:T(8,128)} %copy-done.1) | copy-start | bytes 1572868
  232.6 99.7 %copy-start.4 = (f32[4,128,256]{1,2,0:T(8,128)S(1)}, f32[4,128,256]{1,2,0:T(8,128)}, u32[]{:S(2)}) copy-start(f32[4,128,256]{1,2,0:T(8,128)} %copy-done.3) | copy-start | bytes 1572868
  325.9 10.1 %copy-start.7 = (f32[4,128,256]{2,1,0:T(8,128)S(1)}, f32[4,128,256]{2,1,0:T(8,128)}, u32[]{:S(2)}) copy-start(f32[4,128,256]{2,1,0:T(8,128)} %copy-done.6) | copy-start | bytes 1572868
  325.9 10.1 %copy-start.9 = (f32[4,128,256]{2,1,0:T(8,128)S(1)}, f32[4,128,256]{2,1,0:T(8,128)}, u32[]{:S(2)}) copy-start(f32[4,128,256]{2,1,0:T(8,128)} %copy-done.8) | copy-start | bytes 1572868
  327.7 27.3 %collective-permute-start.4 = (f32[4,128,256]{2,1,0:T(8,128)S(1)}, f32[4,128,256]{2,1,0:T(8,128)S(1)}, u32[]{:S(2)}, u32[]{:S(2)}) collective-permute-start(f32[4,128,256]{2,1,0:T(8,128)S(1)} %fusion.15), channel_id=1, source_target_pairs={{0,16},{16,0},{4,20},{20,4},{8,24},{24,8},{12,28},{28,12},{32,48},... | collective-permute-start | bytes 1572872 | tf_op jit(solution)/shard_map/ppermute | solution.py:30
  355.1 0.8 copy-start.10
  355.1 1.0 copy-start.12
  362.7 94.9 %copy-start.11 = (f32[4,128,256]{2,1,0:T(8,128)S(1)}, f32[4,128,256]{2,1,0:T(8,128)}, u32[]{:S(2)}) copy-start(f32[4,128,256]{2,1,0:T(8,128)} %copy-done.10) | copy-start | bytes 1572868
  362.7 94.9 %copy-start.13 = (f32[4,128,256]{2,1,0:T(8,128)S(1)}, f32[4,128,256]{2,1,0:T(8,128)}, u32[]{:S(2)}) copy-start(f32[4,128,256]{2,1,0:T(8,128)} %copy-done.12) | copy-start | bytes 1572868
Sparse Core Ops, SparseCore 0:
  69.9 34.0 reduce-scatter.1
